TPU v7x, 32 devices: a whole 2x2x4 slice. The times are simulated.
32 devices in a mesh: graph: 16 (over z, y, x), rep: 2 (over core).
Axes of the slice: x: 2, y: 2, z: 4, core: 2. Of those that a mesh axis runs over, the one named last changes fastest.
Arguments:
- grad_out: bfloat16 [8192, 256], P(('graph', 'rep')), may hold values from -6 to 6
- pre_act: bfloat16 [8192, 256], P(('graph', 'rep')), may hold values from -6 to 6
- aggregated: bfloat16 [8192, 256], P(('graph', 'rep')), may hold values from -0.3125 to 0.3125
- weight: bfloat16 [256, 256], replicated, may hold values from -0.375 to 0.375
- adj_tiles: bfloat16 [16, 2, 16, 2, 128, 128], P('graph', 'rep'), may hold values from 0 to 0.039794922
- tile_row: int32 [16, 2, 16, 2], P('graph', 'rep'), may hold values from 0 to 1
- tile_col: int32 [16, 2, 16, 2], P('graph', 'rep'), may hold values from 0 to 3
- tile_count: int32 [16, 2, 16], P('graph', 'rep'), may hold values from 0 to 2, as said below
- node_perm: int32 [16, 512], P('graph'), may hold values from 0 to 511, each once within a row
Outputs:
- input_grad: bfloat16 [8192, 256], P(('graph', 'rep'))
- weight_grad: float32 [256, 256], replicated
- relu_grad: bfloat16 [8192, 256], P(('graph', 'rep'))
Inputs may be any that keep to these rules, and one draw needn't show every extreme that they name: tile_count[g, r, g] is 2 for every partition g and replica r. `node_perm`: each row is a permutation.
All inputs are finite; a program needn't handle non-finite values.
Results may differ from a plain program's by a relative error of at most 0.0049.
Values may be sent and summed in bfloat16 or wider, within the bound.
A program may use at most 128 MiB of HBM per device.

v0:
```python
import jax
import jax.numpy as jnp
from jax import lax
from jax.sharding import PartitionSpec as P


def tile_products(running, sources, row_count, local_tiles, local_row, local_col, local_count):
    piece_parts = sources.shape[0] // row_count
    tile_size = local_tiles.shape[-1]
    feature_width = sources.shape[1]
    blocks = sources.reshape(piece_parts, row_count // tile_size, tile_size, feature_width)
    part_index = jnp.arange(piece_parts, dtype=jnp.int32)
    for slot_index in range(local_tiles.shape[1]):
        chosen = blocks[part_index, local_row[:, slot_index]]
        product = jnp.einsum(
            "kab,kac->kbc", local_tiles[:, slot_index], chosen, preferred_element_type=jnp.float32
        )
        alive = (local_count > slot_index).astype(jnp.float32)
        running = running.at[local_col[:, slot_index]].add(product * alive[:, None, None])
    return running


def body(
    grad_out, pre_act, aggregated, weight, adj_tiles, tile_row, tile_col, tile_count, node_perm
):
    row_count = grad_out.shape[0]
    feature_width = weight.shape[0]
    relu_grad = jnp.where(pre_act > 0, grad_out, jnp.zeros_like(grad_out))
    partial_weight = lax.dot_general(
        aggregated, relu_grad, (((0,), (0,)), ((), ())), preferred_element_type=jnp.float32
    )
    local_tiles = adj_tiles[0, 0]
    local_row = tile_row[0, 0]
    local_col = tile_col[0, 0]
    local_count = tile_count[0, 0]
    local_perm = node_perm[0]
    tile_size = local_tiles.shape[-1]
    col_blocks = lax.axis_size("rep") * (row_count // tile_size)
    empty = jnp.zeros((col_blocks, tile_size, feature_width), jnp.float32)
    back_agg = lax.dot_general(
        relu_grad, weight, (((1,), (1,)), ((), ())), preferred_element_type=jnp.float32
    ).astype(jnp.bfloat16)
    running = tile_products(
        empty,
        lax.all_gather(back_agg, "graph", axis=0, tiled=True),
        row_count,
        local_tiles,
        local_row,
        local_col,
        local_count,
    )
    partial_grad = running.reshape(col_blocks * tile_size, feature_width)
    input_grad = lax.psum_scatter(
        jnp.take(partial_grad, local_perm, axis=0), "rep", scatter_dimension=0, tiled=True
    ).astype(jnp.bfloat16)
    weight_grad = lax.psum(partial_weight, ("graph", "rep"))
    return (input_grad, weight_grad, relu_grad)


def solution(mesh):
    placed = (
        P(("graph", "rep"), None),
        P(("graph", "rep"), None),
        P(("graph", "rep"), None),
        P(),
        P("graph", "rep", None, None, None, None),
        P("graph", "rep", None, None),
        P("graph", "rep", None, None),
        P("graph", "rep", None),
        P("graph", None),
    )
    return jax.shard_map(
        body,
        mesh=mesh,
        in_specs=placed,
        out_specs=(P(("graph", "rep"), None), P(), P(("graph", "rep"), None)),
        check_vma=False,
    )
```

profile of v0, /device:TPU:1, one launch (start us, length us, event | category | flops | bytes accessed | tf_op | source)
XLA Modules:
  0.0 159.6 jit_solution(16786216906860122379)
XLA Ops:
  8.0 0.0 copy-start
  8.0 0.0 copy-start.2
  8.0 0.0 all-gather.2.cloned.1.call-start
  8.1 1.1 compare_select_fusion
  9.2 0.0 copy-start.1
  9.2 0.9 convolution_convert_fusion
  10.0 0.0 all-gather.2.cloned.1.call-update
  10.1 0.0 all-reduce.2.cloned.1.call-start
  10.1 1.8 %convolution_bitcast_fusion = f32[256,256]{0,1:T(8,128)} fusion(bf16[256,256]{1,0:T(8,128)(2,1)S(1)} %compare_select_fusion, bf16[256,256]{1,0:T(8,128)(2,1)} %param.11), kind=kOutput, calls=%fused_computation.7 | convolution fusion | flops 33554432 | bytes 524288 | tf_op jit(solution)/shard_map/dot_general | solution.py:29
  12.0 0.0 all-reduce.2.cloned.1.call-update
  12.0 0.0 reduce-scatter.2.cloned.1.call-start
  12.0 0.7 compare_select_fusion.1
  12.7 0.7 compare_and_fusion
  13.4 0.8 fusion.10
  14.2 0.8 fusion.6
  14.9 0.7 fusion.1
  15.6 0.1 copy.25
  15.7 58.9 %all-gather.2.cloned.1.call-done = bf16[4096,256]{1,0:T(8,128)(2,1)} async-done(((bf16[256,256]{1,0:T(8,128)(2,1)}), bf16[4096,256]{1,0:T(8,128)(2,1)}) %all-gather.2.cloned.1.call-update) | async-done | bytes 2097168 | tf_op jit(solution)/shard_map/all_gather | solution.py:45
  74.6 3.2 %gather_fusion.1 = bf16[16,128,256]{2,1,0:T(8,128)(2,1)} fusion(bf16[16,2,128,256]{3,2,1,0:T(8,128)(2,1)} %bitcast.44, s32[16]{0:T(128)S(1)} %get-tuple-element.9), kind=kCustom, calls=%fused_computation.1 | custom fusion | bytes 2097280 | tf_op jit(solution)/shard_map/gather | solution.py:14
  77.8 2.2 %gather_fusion = bf16[16,128,256]{2,1,0:T(8,128)(2,1)S(1)} fusion(bf16[16,2,128,256]{3,2,1,0:T(8,128)(2,1)} %bitcast.45, s32[16]{0:T(128)S(1)} %get-tuple-element.10), kind=kCustom, calls=%fused_computation | custom fusion | bytes 2097280 | tf_op jit(solution)/shard_map/gather | solution.py:14
  80.1 1.8 %multiply_bitcast_fusion.1 = f32[16,128,256]{1,2,0:T(8,128)} fusion(bf16[16,128,256]{2,1,0:T(8,128)(2,1)S(1)} %gather_fusion, f32[16]{0:T(128)S(1)} %get-tuple-element.14, bf16[16,2,128,128]{3,2,0,1:T(8,128)(2,1)S(1)} %bitcast.42), kind=kOutput, calls=%fused_computation.6 | convolution fusion | flops 134742016 | bytes 3670528 | tf_op jit(solution)/shard_map/kab,kac->kbc/dot_general | solution.py:15
  81.9 1.9 %copy.18 = f32[16,128,256]{2,1,0:T(8,128)S(1)} copy(f32[16,128,256]{1,2,0:T(8,128)} %multiply_bitcast_fusion.1) | data formatting | bytes 4194304 | tf_op jit(solution)/shard_map/mul | solution.py:19
  83.8 3.1 %multiply_bitcast_fusion = f32[16,128,256]{1,2,0:T(8,128)} fusion(bf16[16,128,256]{2,1,0:T(8,128)(2,1)} %gather_fusion.1, f32[16]{0:T(128)S(1)} %get-tuple-element.13, bf16[16,2,128,128]{3,2,0,1:T(8,128)(2,1)S(1)} %bitcast.43), kind=kOutput, calls=%fused_computation.5 | convolution fusion | flops 134742016 | bytes 3670528 | tf_op jit(solution)/shard_map/kab,kac->kbc/dot_general | solution.py:15
  86.9 2.9 %copy.20 = f32[16,128,256]{2,1,0:T(8,128)} copy(f32[16,128,256]{1,2,0:T(8,128)} %multiply_bitcast_fusion) | data formatting | bytes 4194304 | tf_op jit(solution)/shard_map/mul | solution.py:19
  89.8 2.2 %scatter_fusion = f32[4,128,256]{2,1,0:T(8,128)S(1)} fusion(f32[4,128,256]{2,1,0:T(8,128)S(1)} %broadcast_in_dim.10, s32[16]{0:T(128)S(1)} %get-tuple-element.12, f32[16,128,256]{2,1,0:T(8,128)S(1)} %copy.18), kind=kCustom, calls=%fused_computation.3 | custom fusion | flops 524288 | bytes 6291520 | tf_op jit(solution)/shard_map/scatter-add | solution.py:19
  92.0 3.5 %scatter_fusion.1 = f32[4,128,256]{2,1,0:T(8,128)S(1)} fusion(f32[4,128,256]{2,1,0:T(8,128)S(1)} %scatter_fusion, s32[16]{0:T(128)S(1)} %get-tuple-element.11, f32[16,128,256]{2,1,0:T(8,128)} %copy.20), kind=kCustom, calls=%fused_computation.4 | custom fusion | flops 524288 | bytes 6291520 | tf_op jit(solution)/shard_map/scatter-add | solution.py:19
  95.5 1.6 gather_fusion.2
  97.1 0.9 broadcast_select_fusion
  98.0 0.0 reduce-scatter.2.cloned.1.call-update
  98.1 50.6 %all-reduce.2.cloned.1.call-done = f32[256,256]{0,1:T(8,128)} async-done(((f32[256,256]{0,1:T(8,128)}), f32[256,256]{0,1:T(8,128)}) %all-reduce.2.cloned.1.call-update) | async-done | bytes 262160 | tf_op jit(solution)/shard_map/psum | solution.py:56
  148.7 1.8 %copy.21 = f32[256,256]{1,0:T(8,128)} copy(f32[256,256]{0,1:T(8,128)} %all-reduce.2.cloned.1.call-done) | data formatting | bytes 524288
  150.5 1.6 %convert_element_type.31 = bf16[256,256]{1,0:T(8,128)(2,1)} convert(f32[256,256]{1,0:T(8,128)} %reduce-scatter.2.cloned.1.call-done) | non-fusion elementwise | flops 65536 | bytes 393216 | tf_op jit(solution)/shard_map/convert_element_type | solution.py:55
  (6 shorter events, 0.0 us)
Async XLA Ops:
  8.0 1.1 copy-start
  8.0 7.6 %copy-start.2 = (bf16[1,1,16,2,128,128]{5,4,3,2,1,0:T(8,128)(2,1)S(1)}, bf16[1,1,16,2,128,128]{5,4,3,2,1,0:T(8,128)(2,1)}, u32[]{:S(2)}) copy-start(bf16[1,1,16,2,128,128]{5,4,3,2,1,0:T(8,128)(2,1)} %param.13) | copy-start | bytes 3145732
  8.0 66.6 %all-gather.2.cloned.1.call-start = ((), (), s32[]{:S(2)}) async-start(), calls=%async_computation.1 | async-start | bytes 2228224 | tf_op jit(solution)/shard_map/all_gather | solution.py:45
  9.2 68.7 %copy-start.1 = (bf16[256,256]{1,0:T(8,128)(2,1)}, bf16[256,256]{1,0:T(8,128)(2,1)S(1)}, u32[]{:S(2)}) copy-start(bf16[256,256]{1,0:T(8,128)(2,1)S(1)} %compare_select_fusion) | copy-start | bytes 393220
  10.1 138.6 %all-reduce.2.cloned.1.call-start = ((), (), s32[]{:S(2)}) async-start(), calls=%async_computation.3 | async-start | bytes 524288 | tf_op jit(solution)/shard_map/psum | solution.py:56
  12.0 138.5 %reduce-scatter.2.cloned.1.call-start = ((), (), s32[]{:S(2)}) async-start(), calls=%async_computation.2 | async-start | bytes 786432 | tf_op jit(solution)/shard_map/reduce_scatter | solution.py:53
Sparse Core Ops, SparseCore 0:
  12.2 62.3 all-gather.1
  98.2 7.4 reduce-scatter.1
Sparse Core Ops, SparseCore 1:
  17.5 131.1 all-reduce.1
where the time goes:
time: 161 us; the launch traced here: 160 us
  waiting for transfers between devices  110 us (68%)
  between operations  15.6 us (10%)
  local copies, waits for them, and re-layouts  13.7 us (9%)
  other arithmetic  12.9 us (8%)
  matrix products  7.62 us (5%)
    all_gather x1, waiting for transfers between devices, body(): lax.all_gather(back_agg, 'graph', axis=0, tiled=True)  58.9 us
    psum x1, waiting for transfers between devices, body(): weight_grad = lax.psum(partial_weight, ('graph', 'rep'))  50.6 us
    scatter-add x2, other arithmetic, tile_products(): running.at[local_col[:, slot_index]].add(product * alive[:, None, None])  5.68 us
    gather x2, local copies, waits for them, and re-layouts, tile_products(): chosen = blocks[part_index, local_row[:, slot_index]]  5.41 us
    dot_general x2, matrix products, tile_products(): jnp.einsum('kab,kac->kbc', local_tiles[:, slot_index], chosen, preferred_...  4.91 us
    mul x2, local copies, waits for them, and re-layouts, tile_products(): product * alive[:, None, None]  4.82 us
  transfers between devices with their start and end apart: 3, of which 2 were waited for; matrix products, arithmetic and copies ran while one was open for 19% of the time, Pallas kernels for 0%

commit v1 on v0

v1 whole, which is shorter than its diff:
```python
import functools

import jax
import jax.numpy as jnp
from jax import lax
from jax.experimental import pallas as pl
from jax.experimental.pallas import tpu as pltpu
from jax.sharding import PartitionSpec as P

MESH = pl.DeviceIdType.MESH
BF16 = jnp.bfloat16
F32 = jnp.float32
LINE = 4
PLANE = 4


def nearest(z, k):
    if k == 0:
        return z
    low = jnp.where(z < 2, z, 3 - z)
    value = (1 - low) if k == 1 else k
    return jnp.where(z < 2, value, 3 - value)


def fused(
    grad_ref, pre_ref, agg_ref, weight_ref, tiles_hbm, row_ref, col_ref, count_ref, perm_ref,
    input_ref, wgrad_ref, relu_ref,
    blocks, tiles, folded, perm_wide, total, outgoing, incoming,
    w_part, w_pair, w_mine, w_parts, w_done, w_other,
    tile_sem, send_sem, recv_sem, diag_send, diag_recv, w_send, w_recv, pair_send, pair_recv,
):
    parts, rows, width = blocks.shape
    tile = tiles.shape[-1]
    g = lax.axis_index("graph")
    r = lax.axis_index("rep")
    other = 1 - r
    z = g // PLANE
    spot = g - z * PLANE
    y = spot // 2
    x = spot - y * 2
    across_y = (1 - y) * 2 + x
    across_x = y * 2 + (1 - x)
    across_xy = (1 - y) * 2 + (1 - x)

    def peer(k):
        return lax.rem(g + k, parts)

    barrier = pltpu.get_barrier_semaphore()

    def greet(k, carry):
        pl.semaphore_signal(barrier, inc=1, device_id=(peer(k), r), device_id_type=MESH)
        return carry

    lax.fori_loop(1, parts, greet, 0)
    pl.semaphore_signal(barrier, inc=1, device_id=(g, other), device_id_type=MESH)

    load_tiles = pltpu.make_async_copy(tiles_hbm, tiles, tile_sem)
    load_tiles.start()

    grad = grad_ref[...]
    relu_ref[...] = jnp.where(pre_ref[...] > 0, grad, jnp.zeros_like(grad))
    blocks[g] = lax.dot_general(
        relu_ref[...], weight_ref[...], (((1,), (1,)), ((), ())), preferred_element_type=F32
    ).astype(BF16)

    def whole(origin, target, slot, way):
        return pltpu.make_async_remote_copy(
            src_ref=blocks.at[origin],
            dst_ref=blocks.at[origin],
            send_sem=send_sem.at[slot, way],
            recv_sem=recv_sem.at[origin],
            device_id=(target, r),
            device_id_type=MESH,
        )

    def half(k, via):
        zz = nearest(z, k)
        from_here = zz * PLANE + (across_y if via == 0 else across_x)
        part = pl.ds(via * tile, tile)
        return pltpu.make_async_remote_copy(
            src_ref=blocks.at[from_here, part],
            dst_ref=blocks.at[from_here, part],
            send_sem=diag_send.at[via, k],
            recv_sem=diag_recv.at[via, zz],
            device_id=(z * PLANE + (across_x if via == 0 else across_y), r),
            device_id_type=MESH,
        )

    def half_in(k, via):
        zz = nearest(z, k)
        origin = zz * PLANE + across_xy
        part = pl.ds(via * tile, tile)
        return pltpu.make_async_remote_copy(
            src_ref=blocks.at[origin, part],
            dst_ref=blocks.at[origin, part],
            send_sem=diag_send.at[via, k],
            recv_sem=diag_recv.at[via, zz],
            device_id=(z * PLANE + (across_x if via == 0 else across_y), r),
            device_id_type=MESH,
        )

    def along_z(k, act):
        zz = nearest(z, k)
        origin = zz * PLANE + spot
        if k == 0:
            @pl.when(z < LINE - 1)
            def _():
                act(whole(origin, g + PLANE, k, 0))

            @pl.when(z > 0)
            def _():
                act(whole(origin, g - PLANE, k, 1))
        else:
            @pl.when((zz < z) & (z < LINE - 1))
            def _():
                act(whole(origin, g + PLANE, k, 0))

            @pl.when((zz > z) & (z > 0))
            def _():
                act(whole(origin, g - PLANE, k, 1))

    def in_plane(k, act):
        origin = nearest(z, k) * PLANE + spot
        act(whole(origin, z * PLANE + across_y, k, 2))
        act(whole(origin, z * PLANE + across_x, k, 3))

    def start(copy):
        copy.start()

    def wait_sent(copy):
        copy.wait_send()

    def received(origin):
        whole(origin, z * PLANE + across_y, 0, 2).wait_recv()

    def spread(k):
        if k > 0:
            received(nearest(z, k) * PLANE + spot)
        along_z(k, start)
        in_plane(k, start)

    def turn(k):
        zz = nearest(z, k)
        received(zz * PLANE + across_y)
        half(k, 0).start()
        received(zz * PLANE + across_x)
        half(k, 1).start()

    def fold(first, many):
        lanes = lax.broadcasted_iota(jnp.int32, perm_wide.shape, 1)

        def one(p, carry):
            for s in range(2):
                base = jnp.where(count_ref[0, p] > s, col_ref[s, p] * tile, -4 * parts * rows)
                hot = jnp.where(perm_wide[...] == lanes + base, 1.0, 0.0).astype(BF16)
                folded[p, :, s * tile : (s + 1) * tile] = lax.dot_general(
                    hot, tiles[p, s], (((1,), (1,)), ((), ())), preferred_element_type=F32
                ).astype(BF16)
            return carry

        lax.fori_loop(first, first + many, one, 0)

    def chosen(p):
        top = blocks[p, :tile, :]
        low = blocks[p, tile:, :]
        return jnp.concatenate([jnp.where(row_ref[s, p] == 0, top, low) for s in range(2)], axis=0)

    def product(p, side, source):
        return jnp.dot(
            folded[p, pl.ds(side * rows, rows), :], source, preferred_element_type=F32
        )

    def add(p, first=False):
        source = chosen(p)
        for side in range(2):
            if first:
                total[side] = product(p, side, source)
            else:
                total[side] += product(p, side, source)

    def pair(src, dst, which):
        return pltpu.make_async_remote_copy(
            src_ref=src,
            dst_ref=dst,
            send_sem=pair_send.at[which],
            recv_sem=pair_recv.at[which],
            device_id=(g, other),
            device_id_type=MESH,
        )

    def scatter_w(k):
        to = peer(k)
        return pltpu.make_async_remote_copy(
            src_ref=w_mine.at[to],
            dst_ref=w_parts.at[g],
            send_sem=w_send.at[0, k],
            recv_sem=w_recv.at[0, g],
            device_id=(to, r),
            device_id_type=MESH,
        )

    def gather_w(k):
        return pltpu.make_async_remote_copy(
            src_ref=w_done.at[g],
            dst_ref=w_done.at[g],
            send_sem=w_send.at[1, k],
            recv_sem=w_recv.at[1, g],
            device_id=(peer(k), r),
            device_id_type=MESH,
        )

    def wait_w(phase, buffer):
        def one(k, carry):
            origin = peer(k)
            pltpu.make_async_remote_copy(
                src_ref=buffer.at[origin],
                dst_ref=buffer.at[origin],
                send_sem=w_send.at[phase, k],
                recv_sem=w_recv.at[phase, origin],
                device_id=(origin, r),
                device_id_type=MESH,
            ).wait_recv()
            return carry

        lax.fori_loop(1, parts, one, 0)

    def each_peer(make, act):
        def one(k, carry):
            act(make(k))
            return carry

        lax.fori_loop(1, parts, one, 0)

    pl.semaphore_wait(barrier, parts)
    spread(0)

    w_part[...] = lax.dot_general(
        agg_ref[...], relu_ref[...], (((0,), (0,)), ((), ())), preferred_element_type=F32
    ).reshape(w_part.shape)
    w_swap = pair(w_part.at[other], w_pair, 0)
    w_swap.start()

    perm_wide[...] = jnp.broadcast_to(perm_ref[...], (tile, perm_wide.shape[0])).T
    load_tiles.wait()
    fold(0, 2)
    spread(1)

    w_swap.wait_recv()
    w_mine[...] = w_part[r] + w_pair[...]
    each_peer(scatter_w, start)
    w_parts[g] = w_mine[g]
    turn(0)
    fold(2, 4)
    spread(2)
    turn(1)
    wait_w(0, w_parts)
    w_done[g] = jnp.sum(w_parts[...], axis=0)
    each_peer(gather_w, start)
    fold(6, 4)
    spread(3)
    turn(2)
    fold(10, 6)
    turn(3)
    wait_w(1, w_done)
    w_back = pair(w_done, w_other, 1)
    w_back.start()

    add(g, first=True)
    for k in range(1, LINE):
        add(nearest(z, k) * PLANE + spot)
    for k in range(LINE):
        add(nearest(z, k) * PLANE + across_y)
        add(nearest(z, k) * PLANE + across_x)

    w_back.wait_recv()
    w_rows = width // 2
    wgrad_ref[pl.ds(pl.multiple_of(r * w_rows, w_rows), w_rows), :] = w_done[...].reshape(w_rows, width)
    wgrad_ref[pl.ds(pl.multiple_of(other * w_rows, w_rows), w_rows), :] = w_other[...].reshape(w_rows, width)

    for k in range(LINE):
        half_in(k, 0).wait_recv()
        half_in(k, 1).wait_recv()
        p = nearest(z, k) * PLANE + across_xy
        if k < LINE - 1:
            add(p)
    source = chosen(p)
    outgoing[...] = total[other] + product(p, other, source)
    swap = pair(outgoing, incoming, 2)
    swap.start()
    total[r] += product(p, r, source)

    for k in range(LINE):
        along_z(k, wait_sent)
        in_plane(k, wait_sent)
        half(k, 0).wait_send()
        half(k, 1).wait_send()
    each_peer(scatter_w, wait_sent)
    each_peer(gather_w, wait_sent)
    w_swap.wait_send()
    w_back.wait_send()
    swap.wait_recv()
    input_ref[...] = (total[r] + incoming[...]).astype(BF16)
    swap.wait_send()


def fused_body(
    grad_out, pre_act, aggregated, weight, adj_tiles, tile_row, tile_col, tile_count, node_perm
):
    rows, width = grad_out.shape
    parts, slots, tile = adj_tiles.shape[2], adj_tiles.shape[3], adj_tiles.shape[4]
    positions = node_perm.shape[1]
    w_chunk = width // 2 // parts
    vmem = pl.BlockSpec(memory_space=pltpu.VMEM)
    smem = pl.BlockSpec(memory_space=pltpu.SMEM)
    return pl.pallas_call(
        fused,
        out_shape=(
            jax.ShapeDtypeStruct((rows, width), BF16),
            jax.ShapeDtypeStruct((width, width), F32),
            jax.ShapeDtypeStruct((rows, width), BF16),
        ),
        in_specs=[vmem] * 4 + [pl.BlockSpec(memory_space=pl.ANY)] + [smem] * 3 + [vmem],
        out_specs=(vmem, vmem, vmem),
        scratch_shapes=[
            pltpu.VMEM((parts, rows, width), BF16),
            pltpu.VMEM((parts, slots, tile, tile), BF16),
            pltpu.VMEM((parts, positions, slots * tile), BF16),
            pltpu.VMEM((positions, tile), jnp.int32),
            pltpu.VMEM((2, rows, width), F32),
            pltpu.VMEM((rows, width), F32),
            pltpu.VMEM((rows, width), F32),
            pltpu.VMEM((2, parts, w_chunk, width), F32),
            pltpu.VMEM((parts, w_chunk, width), F32),
            pltpu.VMEM((parts, w_chunk, width), F32),
            pltpu.VMEM((parts, w_chunk, width), F32),
            pltpu.VMEM((parts, w_chunk, width), F32),
            pltpu.VMEM((parts, w_chunk, width), F32),
            pltpu.SemaphoreType.DMA,
            pltpu.SemaphoreType.DMA((LINE, 4)),
            pltpu.SemaphoreType.DMA((parts,)),
            pltpu.SemaphoreType.DMA((2, LINE)),
            pltpu.SemaphoreType.DMA((2, LINE)),
            pltpu.SemaphoreType.DMA((2, parts)),
            pltpu.SemaphoreType.DMA((2, parts)),
            pltpu.SemaphoreType.DMA((3,)),
            pltpu.SemaphoreType.DMA((3,)),
        ],
        compiler_params=pltpu.CompilerParams(
            collective_id=0, has_side_effects=True, vmem_limit_bytes=40 * 1024 * 1024
        ),
    )(
        grad_out,
        pre_act,
        aggregated,
        weight,
        adj_tiles.reshape(parts, slots, tile, tile),
        jnp.swapaxes(tile_row[0, 0], 0, 1),
        jnp.swapaxes(tile_col[0, 0], 0, 1),
        tile_count[0],
        node_perm,
    )


def tile_products(running, blocks, local_tiles, local_row, local_col, local_count):
    for slot in range(local_tiles.shape[1]):
        picked = local_row[:, slot][:, None, None]
        chosen = blocks[:, 0]
        for block in range(1, blocks.shape[1]):
            chosen = jnp.where(picked == block, blocks[:, block], chosen)
        product = jnp.einsum(
            "kab,kac->kbc", local_tiles[:, slot], chosen, preferred_element_type=F32
        )
        alive = (local_count > slot).astype(F32)
        running = running.at[local_col[:, slot]].add(product * alive[:, None, None])
    return running


def plain_body(
    grad_out, pre_act, aggregated, weight, adj_tiles, tile_row, tile_col, tile_count, node_perm
):
    row_count, feature_width = grad_out.shape[0], weight.shape[0]
    relu_grad = jnp.where(pre_act > 0, grad_out, jnp.zeros_like(grad_out))
    partial_weight = lax.dot_general(
        aggregated, relu_grad, (((0,), (0,)), ((), ())), preferred_element_type=F32
    )
    local_tiles = adj_tiles[0, 0]
    tile_size = local_tiles.shape[-1]
    row_blocks = row_count // tile_size
    col_blocks = lax.axis_size("rep") * row_blocks
    back_agg = lax.dot_general(
        relu_grad, weight, (((1,), (1,)), ((), ())), preferred_element_type=F32
    ).astype(BF16)
    sources = lax.all_gather(back_agg, "graph", axis=0, tiled=True)
    running = tile_products(
        jnp.zeros((col_blocks, tile_size, feature_width), F32),
        sources.reshape(-1, row_blocks, tile_size, feature_width),
        local_tiles,
        tile_row[0, 0],
        tile_col[0, 0],
        tile_count[0, 0],
    )
    partial_grad = running.reshape(col_blocks * tile_size, feature_width)
    input_grad = lax.psum_scatter(
        jnp.take(partial_grad, node_perm[0], axis=0), "rep", scatter_dimension=0, tiled=True
    ).astype(BF16)
    return (input_grad, lax.psum(partial_weight, ("graph", "rep")), relu_grad)


def solution(mesh):
    placed = (
        P(("graph", "rep"), None),
        P(("graph", "rep"), None),
        P(("graph", "rep"), None),
        P(),
        P("graph", "rep", None, None, None, None),
        P("graph", "rep", None, None),
        P("graph", "rep", None, None),
        P("graph", "rep", None),
        P("graph", None),
    )
    fits = mesh.shape["graph"] == LINE * PLANE and mesh.shape["rep"] == 2
    return jax.shard_map(
        fused_body if fits else plain_body,
        mesh=mesh,
        in_specs=placed,
        out_specs=(P(("graph", "rep"), None), P(), P(("graph", "rep"), None)),
        check_vma=False,
    )
```

time: 161 us -> 43.4 us (0.27)
  waiting for transfers between devices: 110 us -> 0 us
  Pallas kernels: 0 us -> 34.9 us
  between operations: 15.6 us -> 0.68 us
  other arithmetic: 12.9 us -> 0 us
  matrix products: 7.62 us -> 0 us
  local copies, waits for them, and re-layouts: 13.7 us -> 7.54 us
    all_gather x1 -> x0, waiting for transfers between devices: 58.9 us -> none  [body(): lax.all_gather(back_agg, 'graph', axis=0, tiled=True)]
    psum x1 -> x0, waiting for transfers between devices: 50.6 us -> none  [body(): weight_grad = lax.psum(partial_weight, ('graph', 'rep'))]
    pallas_call x0 -> x1, Pallas kernels: none -> 34.9 us  [fused_body(): pl.pallas_call(fused, out_shape=(jax.ShapeDtypeStruct((rows, width), BF16...]
    dot_general x4 -> x0, matrix products: 7.62 us -> none  [the longest x2 4.91 us: tile_products(): jnp.einsum('kab,kac->kbc', local_tiles[:, slot_index], chosen, preferred_...]
    gather x3 -> x0, local copies, waits for them, and re-layouts: 6.98 us -> none  [the longest x2 5.41 us: tile_products(): chosen = blocks[part_index, local_row[:, slot_index]]]
    scatter-add x2 -> x0, other arithmetic: 5.68 us -> none  [tile_products(): running.at[local_col[:, slot_index]].add(product * alive[:, None, None])]
    unnamed x8 -> x21, local copies, waits for them, and re-layouts: 1.91 us -> 7.54 us
    mul x2 -> x0, local copies, waits for them, and re-layouts: 4.82 us -> none  [tile_products(): product * alive[:, None, None]]
  transfers between devices with their start and end apart: 3 -> 0, of which waited for: 2 -> 0; matrix products, arithmetic and copies ran while one was open for 19% -> 0% of each run, Pallas kernels for 0% -> 0%
where the time goes in v1:
time: 43.4 us; the launch traced here: 43.1 us
  Pallas kernels  34.9 us (80%)
  local copies, waits for them, and re-layouts  7.54 us (17%)
  between operations  0.68 us (2%)
    pallas_call x1, Pallas kernels, fused_body(): pl.pallas_call(fused, out_shape=(jax.ShapeDtypeStruct((rows, width), BF16...  34.9 us
    unnamed x21, local copies, waits for them, and re-layouts  7.54 us

profile of v1, /device:TPU:1, one launch (start us, length us, event | category | flops | bytes accessed | tf_op | source)
XLA Modules:
  0.0 43.1 jit_solution(15522343070629512029)
XLA Ops:
  0.6 0.0 copy-start.7
  0.6 0.0 copy-start.5
  0.7 0.0 copy-start.6
  0.7 0.0 copy-start.8
  0.7 0.6 %copy-done.7 = s32[1,1,16,2]{2,3,1,0:T(2,128)S(1)} copy-done((s32[1,1,16,2]{2,3,1,0:T(2,128)S(1)}, s32[1,1,16,2]{2,3,1,0:T(2,128)}, u32[]{:S(2)}) %copy-start.7) | copy-done | bytes 152
  1.3 0.0 copy-done.5
  1.3 0.0 copy-done.6
  1.3 0.0 copy-done.8
  1.3 0.0 copy-start
  1.4 1.2 %copy-done = bf16[1,1,16,2,128,128]{5,4,3,2,1,0:T(8,128)(2,1)S(1)} copy-done((bf16[1,1,16,2,128,128]{5,4,3,2,1,0:T(8,128)(2,1)S(1)}, bf16[1,1,16,2,128,128]{5,4,3,2,1,0:T(8,128)(2,1)}, u32[]{:S(2)}) %copy-start) | copy-done | bytes 1048600
  2.6 0.0 copy-start.1
  2.6 0.9 %copy-done.1 = bf16[256,256]{1,0:T(8,128)(2,1)S(1)} copy-done((bf16[256,256]{1,0:T(8,128)(2,1)S(1)}, bf16[256,256]{1,0:T(8,128)(2,1)}, u32[]{:S(2)}) %copy-start.1) | copy-done | bytes 131096
  3.5 0.0 copy-start.2
  3.5 0.9 %copy-done.2 = bf16[256,256]{1,0:T(8,128)(2,1)S(1)} copy-done((bf16[256,256]{1,0:T(8,128)(2,1)S(1)}, bf16[256,256]{1,0:T(8,128)(2,1)}, u32[]{:S(2)}) %copy-start.2) | copy-done | bytes 131096
  4.4 0.0 copy-start.3
  4.4 0.9 %copy-done.3 = bf16[256,256]{1,0:T(8,128)(2,1)S(1)} copy-done((bf16[256,256]{1,0:T(8,128)(2,1)S(1)}, bf16[256,256]{1,0:T(8,128)(2,1)}, u32[]{:S(2)}) %copy-start.3) | copy-done | bytes 131096
  5.3 0.0 copy-start.4
  5.3 0.9 %copy-done.4 = bf16[256,256]{1,0:T(8,128)(2,1)S(1)} copy-done((bf16[256,256]{1,0:T(8,128)(2,1)S(1)}, bf16[256,256]{1,0:T(8,128)(2,1)}, u32[]{:S(2)}) %copy-start.4) | copy-done | bytes 131096
  6.2 34.9 %shard_map.112 = (bf16[256,256]{1,0:T(8,128)(2,1)S(1)}, f32[256,256]{1,0:T(8,128)S(1)}, bf16[256,256]{1,0:T(8,128)(2,1)S(1)}) custom-call(bf16[256,256]{1,0:T(8,128)(2,1)S(1)} %copy-done.1, bf16[256,256]{1,0:T(8,128)(2,1)S(1)} %copy-done.2, bf16[256,256]{1,0:T(8,128)(2,1)S(1)} %copy-done.3, bf16[256,256]{1,0:T(8,128)(2,1)S(1)} %copy-done.4, ...), custom_call_target="tpu_custom_call" | custom-call | tf_op jit(solution)/shard_map/pallas_call | solution.py:315
  41.1 0.7 %copy.15 = bf16[256,256]{1,0:T(8,128)(2,1)} copy(bf16[256,256]{1,0:T(8,128)(2,1)S(1)} %get-tuple-element.6) | data formatting | bytes 262144
  41.8 0.7 %copy.16 = f32[256,256]{1,0:T(8,128)} copy(f32[256,256]{1,0:T(8,128)S(1)} %get-tuple-element.7) | data formatting | bytes 524288
  42.5 0.7 %copy.17 = bf16[256,256]{1,0:T(8,128)(2,1)} copy(bf16[256,256]{1,0:T(8,128)(2,1)S(1)} %get-tuple-element.8) | data formatting | bytes 262144
Async XLA Ops:
  0.6 0.7 %copy-start.7 = (s32[1,1,16,2]{2,3,1,0:T(2,128)S(1)}, s32[1,1,16,2]{2,3,1,0:T(2,128)}, u32[]{:S(2)}) copy-start(s32[1,1,16,2]{2,3,1,0:T(2,128)} %param.15) | copy-start | bytes 388
  0.6 0.7 %copy-start.5 = (s32[1,512]{1,0:T(1,128)S(1)}, s32[1,512]{1,0:T(1,128)}, u32[]{:S(2)}) copy-start(s32[1,512]{1,0:T(1,128)} %perm_ref.1) | copy-start | bytes 6148
  0.7 0.7 %copy-start.6 = (s32[1,1,16,2]{2,3,1,0:T(2,128)S(1)}, s32[1,1,16,2]{2,3,1,0:T(2,128)}, u32[]{:S(2)}) copy-start(s32[1,1,16,2]{2,3,1,0:T(2,128)} %param.14) | copy-start | bytes 388
  0.7 0.7 %copy-start.8 = (s32[1,1,16]{2,1,0:T(1,128)S(1)}, s32[1,1,16]{2,1,0:T(1,128)}, u32[]{:S(2)}) copy-start(s32[1,1,16]{2,1,0:T(1,128)} %param.16) | copy-start | bytes 196
  1.3 1.2 %copy-start = (bf16[1,1,16,2,128,128]{5,4,3,2,1,0:T(8,128)(2,1)S(1)}, bf16[1,1,16,2,128,128]{5,4,3,2,1,0:T(8,128)(2,1)}, u32[]{:S(2)}) copy-start(bf16[1,1,16,2,128,128]{5,4,3,2,1,0:T(8,128)(2,1)} %param.13) | copy-start | bytes 3145732
  2.6 0.9 %copy-start.1 = (bf16[256,256]{1,0:T(8,128)(2,1)S(1)}, bf16[256,256]{1,0:T(8,128)(2,1)}, u32[]{:S(2)}) copy-start(bf16[256,256]{1,0:T(8,128)(2,1)} %grad_ref.1) | copy-start | bytes 393220
  3.5 0.9 %copy-start.2 = (bf16[256,256]{1,0:T(8,128)(2,1)S(1)}, bf16[256,256]{1,0:T(8,128)(2,1)}, u32[]{:S(2)}) copy-start(bf16[256,256]{1,0:T(8,128)(2,1)} %pre_ref.1) | copy-start | bytes 393220
  4.4 0.9 %copy-start.3 = (bf16[256,256]{1,0:T(8,128)(2,1)S(1)}, bf16[256,256]{1,0:T(8,128)(2,1)}, u32[]{:S(2)}) copy-start(bf16[256,256]{1,0:T(8,128)(2,1)} %agg_ref.1) | copy-start | bytes 393220
  5.3 0.9 %copy-start.4 = (bf16[256,256]{1,0:T(8,128)(2,1)S(1)}, bf16[256,256]{1,0:T(8,128)(2,1)}, u32[]{:S(2)}) copy-start(bf16[256,256]{1,0:T(8,128)(2,1)} %weight_ref.1) | copy-start | bytes 393220

commit v2 on v1

--- a/solution.py
+++ b/solution.py
@@ -23,11 +23,13 @@
 
 
 def fused(
-    grad_ref, pre_ref, agg_ref, weight_ref, tiles_hbm, row_ref, col_ref, count_ref, perm_ref,
-    input_ref, wgrad_ref, relu_ref,
+    grad_hbm, pre_hbm, agg_hbm, weight_hbm, tiles_hbm, row_hbm, col_hbm, count_hbm, perm_hbm,
+    input_hbm, wgrad_hbm, relu_hbm,
+    input_ref, wgrad_ref, relu_ref, store_sem,
+    grad_ref, pre_ref, agg_ref, weight_ref, row_ref, col_ref, count_ref, perm_ref, load_sem,
     blocks, tiles, folded, perm_wide, total, outgoing, incoming,
     w_part, w_pair, w_mine, w_parts, w_done, w_other,
-    tile_sem, send_sem, recv_sem, diag_send, diag_recv, w_send, w_recv, pair_send, pair_recv,
+    send_sem, recv_sem, diag_send, diag_recv, w_send, w_recv, pair_send, pair_recv,
 ):
     parts, rows, width = blocks.shape
     tile = tiles.shape[-1]
@@ -45,6 +47,21 @@
     def peer(k):
         return lax.rem(g + k, parts)
 
+    loads = [
+        pltpu.make_async_copy(src, dst, load_sem.at[i])
+        for i, (src, dst) in enumerate((
+            (grad_hbm, grad_ref), (pre_hbm, pre_ref), (weight_hbm, weight_ref), (agg_hbm, agg_ref),
+            (perm_hbm, perm_ref), (count_hbm, count_ref), (col_hbm, col_ref), (row_hbm, row_ref),
+            (tiles_hbm, tiles),
+        ))
+    ]
+    for load in loads[:4]:
+        load.start()
+
+    store_input = pltpu.make_async_copy(input_ref, input_hbm, store_sem.at[0])
+    store_wgrad = pltpu.make_async_copy(wgrad_ref, wgrad_hbm, store_sem.at[1])
+    store_relu = pltpu.make_async_copy(relu_ref, relu_hbm, store_sem.at[2])
+
     barrier = pltpu.get_barrier_semaphore()
 
     def greet(k, carry):
@@ -54,8 +71,10 @@
     lax.fori_loop(1, parts, greet, 0)
     pl.semaphore_signal(barrier, inc=1, device_id=(g, other), device_id_type=MESH)
 
-    load_tiles = pltpu.make_async_copy(tiles_hbm, tiles, tile_sem)
-    load_tiles.start()
+    for load in loads[4:]:
+        load.start()
+    for load in loads[:3]:
+        load.wait()
 
     grad = grad_ref[...]
     relu_ref[...] = jnp.where(pre_ref[...] > 0, grad, jnp.zeros_like(grad))
@@ -233,7 +252,10 @@
 
     pl.semaphore_wait(barrier, parts)
     spread(0)
-
+    store_relu.start()
+
+    for load in loads[3:]:
+        load.wait()
     w_part[...] = lax.dot_general(
         agg_ref[...], relu_ref[...], (((0,), (0,)), ((), ())), preferred_element_type=F32
     ).reshape(w_part.shape)
@@ -241,7 +263,6 @@
     w_swap.start()
 
     perm_wide[...] = jnp.broadcast_to(perm_ref[...], (tile, perm_wide.shape[0])).T
-    load_tiles.wait()
     fold(0, 2)
     spread(1)
 
@@ -276,6 +297,7 @@
     w_rows = width // 2
     wgrad_ref[pl.ds(pl.multiple_of(r * w_rows, w_rows), w_rows), :] = w_done[...].reshape(w_rows, width)
     wgrad_ref[pl.ds(pl.multiple_of(other * w_rows, w_rows), w_rows), :] = w_other[...].reshape(w_rows, width)
+    store_wgrad.start()
 
     for k in range(LINE):
         half_in(k, 0).wait_recv()
@@ -300,7 +322,21 @@
     w_back.wait_send()
     swap.wait_recv()
     input_ref[...] = (total[r] + incoming[...]).astype(BF16)
+    store_input.start()
     swap.wait_send()
+    store_relu.wait()
+    store_wgrad.wait()
+    store_input.wait()
+
+
+def write_out(*refs):
+    copies = [
+        pltpu.make_async_copy(refs[i], refs[3 + i], refs[6].at[i]) for i in range(3)
+    ]
+    for copy in copies:
+        copy.start()
+    for copy in copies:
+        copy.wait()
 
 
 def fused_body(
@@ -310,18 +346,32 @@
     parts, slots, tile = adj_tiles.shape[2], adj_tiles.shape[3], adj_tiles.shape[4]
     positions = node_perm.shape[1]
     w_chunk = width // 2 // parts
-    vmem = pl.BlockSpec(memory_space=pltpu.VMEM)
-    smem = pl.BlockSpec(memory_space=pltpu.SMEM)
-    return pl.pallas_call(
+    anywhere = pl.BlockSpec(memory_space=pl.ANY)
+    hbm = pl.BlockSpec(memory_space=pltpu.HBM)
+    results = (
+        jax.ShapeDtypeStruct((rows, width), BF16),
+        jax.ShapeDtypeStruct((width, width), F32),
+        jax.ShapeDtypeStruct((rows, width), BF16),
+    )
+    made = pl.pallas_call(
         fused,
-        out_shape=(
-            jax.ShapeDtypeStruct((rows, width), BF16),
-            jax.ShapeDtypeStruct((width, width), F32),
-            jax.ShapeDtypeStruct((rows, width), BF16),
-        ),
-        in_specs=[vmem] * 4 + [pl.BlockSpec(memory_space=pl.ANY)] + [smem] * 3 + [vmem],
-        out_specs=(vmem, vmem, vmem),
+        out_shape=results,
+        in_specs=[hbm] * 9,
+        out_specs=(hbm, hbm, hbm),
         scratch_shapes=[
+            pltpu.VMEM((rows, width), BF16),
+            pltpu.VMEM((width, width), F32),
+            pltpu.VMEM((rows, width), BF16),
+            pltpu.SemaphoreType.DMA((3,)),
+            pltpu.VMEM((rows, width), BF16),
+            pltpu.VMEM((rows, width), BF16),
+            pltpu.VMEM((rows, width), BF16),
+            pltpu.VMEM((width, width), BF16),
+            pltpu.SMEM((slots, parts), jnp.int32),
+            pltpu.SMEM((slots, parts), jnp.int32),
+            pltpu.SMEM((1, parts), jnp.int32),
+            pltpu.VMEM((1, positions), jnp.int32),
+            pltpu.SemaphoreType.DMA((9,)),
             pltpu.VMEM((parts, rows, width), BF16),
             pltpu.VMEM((parts, slots, tile, tile), BF16),
             pltpu.VMEM((parts, positions, slots * tile), BF16),
@@ -335,7 +385,6 @@
             pltpu.VMEM((parts, w_chunk, width), F32),
             pltpu.VMEM((parts, w_chunk, width), F32),
             pltpu.VMEM((parts, w_chunk, width), F32),
-            pltpu.SemaphoreType.DMA,
             pltpu.SemaphoreType.DMA((LINE, 4)),
             pltpu.SemaphoreType.DMA((parts,)),
             pltpu.SemaphoreType.DMA((2, LINE)),
@@ -346,7 +395,7 @@
             pltpu.SemaphoreType.DMA((3,)),
         ],
         compiler_params=pltpu.CompilerParams(
-            collective_id=0, has_side_effects=True, vmem_limit_bytes=40 * 1024 * 1024
+            collective_id=0, has_side_effects=True, vmem_limit_bytes=60 * 1024 * 1024
         ),
     )(
         grad_out,
@@ -359,6 +408,14 @@
         tile_count[0],
         node_perm,
     )
+    return pl.pallas_call(
+        write_out,
+        out_shape=results,
+        in_specs=[anywhere] * 3,
+        out_specs=(hbm, hbm, hbm),
+        scratch_shapes=[pltpu.SemaphoreType.DMA((3,))],
+        compiler_params=pltpu.CompilerParams(vmem_limit_bytes=60 * 1024 * 1024),
+    )(*made)
 
 
 def tile_products(running, blocks, local_tiles, local_row, local_col, local_count):

time: 43.4 us -> 52.4 us (1.21)
  Pallas kernels: 34.9 us -> 51.6 us
  local copies, waits for them, and re-layouts: 7.54 us -> 0 us
    pallas_call x1 -> x2, Pallas kernels: 34.9 us -> 51.6 us  [the longest x1 34.6 us: fused_body(): pl.pallas_call(fused, out_shape=results, in_specs=[hbm] * 9, out_specs=(h...]
    unnamed x21 -> x0, local copies, waits for them, and re-layouts: 7.54 us -> none
where the time goes in v2:
time: 52.4 us; the launch traced here: 52.3 us
  Pallas kernels  51.6 us (98%)
  between operations  0.64 us (1%)
    pallas_call x1, Pallas kernels, fused_body(): pl.pallas_call(fused, out_shape=results, in_specs=[hbm] * 9, out_specs=(h...  34.6 us
    pallas_call x1, Pallas kernels, fused_body(): pl.pallas_call(write_out, out_shape=results, in_specs=[anywhere] * 3, out...  17 us

profile of v2, /device:TPU:1, one launch (start us, length us, event | category | flops | bytes accessed | tf_op | source)
XLA Modules:
  0.0 52.3 jit_solution(3974861570383497957)
XLA Ops:
  0.6 34.6 %shard_map.112 = (bf16[256,256]{1,0:T(8,128)(2,1)}, f32[256,256]{1,0:T(8,128)}, bf16[256,256]{1,0:T(8,128)(2,1)}) custom-call(bf16[256,256]{1,0:T(8,128)(2,1)} %grad_hbm.1, bf16[256,256]{1,0:T(8,128)(2,1)} %pre_hbm.1, bf16[256,256]{1,0:T(8,128)(2,1)} %agg_hbm.1, bf16[256,256]{1,0:T(8,128)(2,1)} %weight_hbm.1, bf16[16,2,128,128]{3,2,1,0:T(8,128)(2,1)} %bitcast.8, ...), custom_call_target="tpu_custom_call" | custom-call | tf_op jit(solution)/shard_map/pallas_call | solution.py:356
  35.3 17.0 %shard_map.113 = (bf16[256,256]{1,0:T(8,128)(2,1)}, f32[256,256]{1,0:T(8,128)}, bf16[256,256]{1,0:T(8,128)(2,1)}) custom-call(bf16[256,256]{1,0:T(8,128)(2,1)} %get-tuple-element.6.refs_0_, f32[256,256]{1,0:T(8,128)} %get-tuple-element.7.refs_1_, bf16[256,256]{1,0:T(8,128)(2,1)} %get-tuple-element.8.refs_2_), custom_call_target="tpu_custom_call" | custom-call | tf_op jit(solution)/shard_map/pallas_call | solution.py:411

commit v3 on v2

--- a/solution.py
+++ b/solution.py
@@ -330,13 +330,16 @@
 
 
 def write_out(*refs):
-    copies = [
-        pltpu.make_async_copy(refs[i], refs[3 + i], refs[6].at[i]) for i in range(3)
-    ]
-    for copy in copies:
-        copy.start()
-    for copy in copies:
-        copy.wait()
+    made, results, held, sems = refs[:3], refs[3:6], refs[6:9], refs[9]
+    reads = [pltpu.make_async_copy(made[i], held[i], sems.at[0, i]) for i in range(3)]
+    writes = [pltpu.make_async_copy(held[i], results[i], sems.at[1, i]) for i in range(3)]
+    for read in reads:
+        read.start()
+    for read, write in zip(reads, writes):
+        read.wait()
+        write.start()
+    for write in writes:
+        write.wait()
 
 
 def fused_body(
@@ -413,7 +416,8 @@
         out_shape=results,
         in_specs=[anywhere] * 3,
         out_specs=(hbm, hbm, hbm),
-        scratch_shapes=[pltpu.SemaphoreType.DMA((3,))],
+        scratch_shapes=[pltpu.VMEM(made_one.shape, made_one.dtype) for made_one in results]
+        + [pltpu.SemaphoreType.DMA((2, 3))],
         compiler_params=pltpu.CompilerParams(vmem_limit_bytes=60 * 1024 * 1024),
     )(*made)
 

time: 52.4 us -> 37.2 us (0.71)
  Pallas kernels: 51.6 us -> 36.4 us
    pallas_call x1, Pallas kernels: 17 us -> 1.81 us  [fused_body(): pl.pallas_call(write_out, out_shape=results, in_specs=[anywhere] * 3, out...]
where the time goes in v3:
time: 37.2 us; the launch traced here: 37.1 us
  Pallas kernels  36.4 us (98%)
  between operations  0.64 us (2%)
    pallas_call x1, Pallas kernels, fused_body(): pl.pallas_call(fused, out_shape=results, in_specs=[hbm] * 9, out_specs=(h...  34.6 us
    pallas_call x1, Pallas kernels, fused_body(): pl.pallas_call(write_out, out_shape=results, in_specs=[anywhere] * 3, out...  1.81 us

profile of v3, /device:TPU:1, one launch (start us, length us, event | category | flops | bytes accessed | tf_op | source)
XLA Modules:
  0.0 37.1 jit_solution(10522310332726990876)
XLA Ops:
  0.6 34.6 %shard_map.112 = (bf16[256,256]{1,0:T(8,128)(2,1)}, f32[256,256]{1,0:T(8,128)}, bf16[256,256]{1,0:T(8,128)(2,1)}) custom-call(bf16[256,256]{1,0:T(8,128)(2,1)} %grad_hbm.1, bf16[256,256]{1,0:T(8,128)(2,1)} %pre_hbm.1, bf16[256,256]{1,0:T(8,128)(2,1)} %agg_hbm.1, bf16[256,256]{1,0:T(8,128)(2,1)} %weight_hbm.1, bf16[16,2,128,128]{3,2,1,0:T(8,128)(2,1)} %bitcast.8, ...), custom_call_target="tpu_custom_call" | custom-call | tf_op jit(solution)/shard_map/pallas_call | solution.py:359
  35.3 1.8 %shard_map.113 = (bf16[256,256]{1,0:T(8,128)(2,1)}, f32[256,256]{1,0:T(8,128)}, bf16[256,256]{1,0:T(8,128)(2,1)}) custom-call(bf16[256,256]{1,0:T(8,128)(2,1)} %get-tuple-element.6.refs_0_, f32[256,256]{1,0:T(8,128)} %get-tuple-element.7.refs_1_, bf16[256,256]{1,0:T(8,128)(2,1)} %get-tuple-element.8.refs_2_), custom_call_target="tpu_custom_call" | custom-call | tf_op jit(solution)/shard_map/pallas_call | solution.py:414
